TPU v7x, 512 devices: a whole 4x4x16 slice. The times are simulated.
512 devices in a mesh: head: 8 (over y_lo, x), blk: 64 (over z, y_hi, core).
Axes of the slice: x: 4, y: 4 (y_hi: 2, y_lo: 2; y = y_hi * 2 + y_lo), z: 16, core: 2. Of those that a mesh axis runs over, the one named last changes fastest.
Arguments:
- query_rows: bfloat16 [32768, 2048], P(('blk', 'head')), may hold values from -128 to 128, as said below
- key_rows: bfloat16 [32768, 2048], P(('blk', 'head')), may hold values from -4 to 4
- value_rows: bfloat16 [32768, 2048], P(('blk', 'head')), may hold values from -6 to 6
- grad_out: bfloat16 [32768, 2048], P(('blk', 'head')), may hold values from -6 to 6
Outputs:
- attended: bfloat16 [32768, 2048], P(('blk', 'head'))
- grad_query: bfloat16 [32768, 2048], P(('blk', 'head'))
- grad_key: bfloat16 [32768, 2048], P(('blk', 'head'))
- grad_value: bfloat16 [32768, 2048], P(('blk', 'head'))
Inputs may be any that keep to these rules, and one draw needn't show every extreme that they name: `query_rows`: a few query rows may be large, with scores up to about 300.
All inputs are finite; a program needn't handle non-finite values.
Results may differ from a plain program's by a relative error of at most 0.035.
Values may be sent and summed in bfloat16 or wider, within the bound.
A program may use at most 64 MiB of HBM per device.

v0:
```python
import math

import jax
import jax.numpy as jnp
from jax import lax
from jax.sharding import PartitionSpec as P

DH = 128


def passed_along(value, axis, by):
    size = lax.axis_size(axis)
    pairs = [(i, i + by) for i in range(size) if 0 <= i + by < size]
    return lax.ppermute(value, axis, pairs)


def times_transposed(lhs_matrix, rhs_matrix):
    return lax.dot_general(
        lhs_matrix, rhs_matrix, (((1,), (1,)), ((), ())), preferred_element_type=jnp.float32
    )


def transposed_times(lhs_matrix, rhs_matrix):
    return lax.dot_general(
        lhs_matrix, rhs_matrix, (((0,), (0,)), ((), ())), preferred_element_type=jnp.float32
    )


def on_device(query_rows, key_rows, value_rows, grad_out):
    scaling = 1.0 / math.sqrt(DH)
    queries, key_block, value_block, grads = (
        lax.all_to_all(query_rows, "head", split_axis=1, concat_axis=0, tiled=True),
        lax.all_to_all(key_rows, "head", split_axis=1, concat_axis=0, tiled=True),
        lax.all_to_all(value_rows, "head", split_axis=1, concat_axis=0, tiled=True),
        lax.all_to_all(grad_out, "head", split_axis=1, concat_axis=0, tiled=True),
    )
    lower_keys, lower_values = passed_along((key_block, value_block), "blk", 1)
    upper_keys, upper_values = passed_along((key_block, value_block), "blk", -1)
    window_keys = jnp.concatenate([lower_keys, key_block, upper_keys], axis=0)
    window_values = jnp.concatenate([lower_values, value_block, upper_values], axis=0)
    seg_rows = queries.shape[0]
    heads_here = queries.shape[1] // DH
    position = lax.axis_index("blk")
    count = lax.axis_size("blk")
    valid = jnp.concatenate(
        [
            jnp.full((seg_rows,), position > 0),
            jnp.full((seg_rows,), True),
            jnp.full((seg_rows,), position < count - 1),
        ],
        axis=0,
    )
    outputs, query_grads, totals, delta_list, key_parts, value_parts = ([], [], [], [], [], [])
    for head_index in range(heads_here):
        columns = slice(head_index * DH, (head_index + 1) * DH)
        query_head = queries[:, columns]
        key_head = window_keys[:, columns]
        value_head = window_values[:, columns]
        grad_head = grads[:, columns]
        scores = times_transposed(query_head, key_head) * scaling
        scores = jnp.where(valid[None, :], scores, -jnp.inf)
        row_top = jnp.max(scores, axis=1, keepdims=True)
        log_total = row_top + jnp.log(jnp.sum(jnp.exp(scores - row_top), axis=1, keepdims=True))
        probs = jnp.exp(scores - log_total)
        probs_low = probs.astype(jnp.bfloat16)
        output_head = jnp.dot(probs_low, value_head, preferred_element_type=jnp.float32).astype(
            jnp.bfloat16
        )
        deltas = jnp.sum(grad_head.astype(jnp.float32) * output_head.astype(jnp.float32), axis=1)
        dprobs = times_transposed(grad_head, value_head)
        dscores = (probs * (dprobs - deltas[:, None]) * scaling).astype(jnp.bfloat16)
        query_grads.append(
            jnp.dot(dscores, key_head, preferred_element_type=jnp.float32).astype(jnp.bfloat16)
        )
        outputs.append(output_head)
        totals.append(log_total[:, 0])
        delta_list.append(deltas)
        key_parts.append(transposed_times(dscores, query_head))
        value_parts.append(transposed_times(probs_low, grad_head))
    attended = jnp.concatenate(outputs, axis=1)
    grad_query = jnp.concatenate(query_grads, axis=1)
    key_terms = jnp.concatenate(key_parts, axis=1)
    value_terms = jnp.concatenate(value_parts, axis=1)
    upper_key_terms, upper_value_terms = passed_along(
        (key_terms[:seg_rows], value_terms[:seg_rows]), "blk", -1
    )
    lower_key_terms, lower_value_terms = passed_along(
        (key_terms[2 * seg_rows :], value_terms[2 * seg_rows :]), "blk", 1
    )
    grad_key = (key_terms[seg_rows : 2 * seg_rows] + upper_key_terms + lower_key_terms).astype(
        jnp.bfloat16
    )
    grad_value = (
        value_terms[seg_rows : 2 * seg_rows] + upper_value_terms + lower_value_terms
    ).astype(jnp.bfloat16)
    return (
        lax.all_to_all(attended, "head", split_axis=0, concat_axis=1, tiled=True),
        lax.all_to_all(grad_query, "head", split_axis=0, concat_axis=1, tiled=True),
        lax.all_to_all(grad_key, "head", split_axis=0, concat_axis=1, tiled=True),
        lax.all_to_all(grad_value, "head", split_axis=0, concat_axis=1, tiled=True),
    )


def solution(mesh):
    in_specs = (
        P(("blk", "head"), None),
        P(("blk", "head"), None),
        P(("blk", "head"), None),
        P(("blk", "head"), None),
    )
    out_specs = (
        P(("blk", "head"), None),
        P(("blk", "head"), None),
        P(("blk", "head"), None),
        P(("blk", "head"), None),
    )
    return jax.shard_map(
        on_device, mesh=mesh, in_specs=in_specs, out_specs=out_specs, check_vma=False
    )
```

profile of v0, /device:TPU:1, one launch (start us, length us, event | category | flops | bytes accessed | tf_op | source)
XLA Modules:
  0.0 133.2 jit_solution(14207466977671724131)
XLA Ops:
  0.6 1.7 %copy.64 = bf16[8,8,8,256]{3,2,0,1:T(8,128)(2,1)} copy(bf16[8,8,8,256]{3,2,1,0:T(8,128)(2,1)} %bitcast.68) | data formatting | bytes 524288 | tf_op jit(solution)/shard_map/all_to_all | solution.py:33
  2.4 5.9 %all-to-all-start = ((bf16[64,8,256]{2,0,1:T(8,128)(2,1)}), bf16[64,8,256]{2,0,1:T(8,128)(2,1)S(1)}, u32[]{:S(2)}, u32[]{:S(2)}) async-start(bf16[64,8,256]{2,0,1:T(8,128)(2,1)} %bitcast.47), calls=%async_computation | async-start | bytes 524288 | tf_op jit(solution)/shard_map/all_to_all | solution.py:33
  8.2 1.7 %copy.62 = bf16[8,8,8,256]{3,2,0,1:T(8,128)(2,1)} copy(bf16[8,8,8,256]{3,2,1,0:T(8,128)(2,1)} %bitcast.69) | data formatting | bytes 524288 | tf_op jit(solution)/shard_map/all_to_all | solution.py:34
  9.9 4.5 %all-to-all-done = bf16[64,8,256]{2,0,1:T(8,128)(2,1)S(1)} async-done(((bf16[64,8,256]{2,0,1:T(8,128)(2,1)}), bf16[64,8,256]{2,0,1:T(8,128)(2,1)S(1)}, u32[]{:S(2)}, u32[]{:S(2)}) %all-to-all-start) | async-done | bytes 262176 | tf_op jit(solution)/shard_map/all_to_all | solution.py:33
  14.4 3.4 %all-to-all-start.2 = ((bf16[64,8,256]{2,0,1:T(8,128)(2,1)}), bf16[64,8,256]{2,0,1:T(8,128)(2,1)S(1)}, u32[]{:S(2)}, u32[]{:S(2)}) async-start(bf16[64,8,256]{2,0,1:T(8,128)(2,1)} %bitcast.45), calls=%async_computation.2 | async-start | bytes 524288 | tf_op jit(solution)/shard_map/all_to_all | solution.py:34
  17.8 1.7 %copy.61 = bf16[8,8,8,256]{3,2,0,1:T(8,128)(2,1)} copy(bf16[8,8,8,256]{3,2,1,0:T(8,128)(2,1)} %bitcast.70) | data formatting | bytes 524288 | tf_op jit(solution)/shard_map/all_to_all | solution.py:35
  19.4 4.4 %all-to-all-done.2 = bf16[64,8,256]{2,0,1:T(8,128)(2,1)S(1)} async-done(((bf16[64,8,256]{2,0,1:T(8,128)(2,1)}), bf16[64,8,256]{2,0,1:T(8,128)(2,1)S(1)}, u32[]{:S(2)}, u32[]{:S(2)}) %all-to-all-start.2) | async-done | bytes 262176 | tf_op jit(solution)/shard_map/all_to_all | solution.py:34
  23.8 3.4 %all-to-all-start.4 = ((bf16[64,8,256]{2,0,1:T(8,128)(2,1)}), bf16[64,8,256]{2,0,1:T(8,128)(2,1)S(1)}, u32[]{:S(2)}, u32[]{:S(2)}) async-start(bf16[64,8,256]{2,0,1:T(8,128)(2,1)} %bitcast.44), calls=%async_computation.4 | async-start | bytes 524288 | tf_op jit(solution)/shard_map/all_to_all | solution.py:35
  27.3 8.6 %collective-permute-start.1 = (bf16[512,256]{1,0:T(8,128)(2,1)S(1)}, bf16[512,256]{1,0:T(8,128)(2,1)S(1)}, u32[]{:S(2)}, u32[]{:S(2)}) collective-permute-start(bf16[512,256]{1,0:T(8,128)(2,1)S(1)} %bitcast.65), channel_id=1, source_target_pairs={{1,0},{2,1},{3,2},{4,3},{5,4},{6,5},{7,6},{8,7},{9,8},{10,9},{11,1... | collective-permute-start | bytes 786440 | tf_op jit(solution)/shard_map/ppermute | solution.py:14
  35.9 1.9 %collective-permute-start = (bf16[512,256]{1,0:T(8,128)(2,1)S(1)}, bf16[512,256]{1,0:T(8,128)(2,1)S(1)}, u32[]{:S(2)}, u32[]{:S(2)}) collective-permute-start(bf16[512,256]{1,0:T(8,128)(2,1)S(1)} %bitcast.66), channel_id=1, source_target_pairs={{0,1},{1,2},{2,3},{3,4},{4,5},{5,6},{6,7},{7,8},{8,9},{9,10},{10,1... | collective-permute-start | bytes 786440 | tf_op jit(solution)/shard_map/ppermute | solution.py:14
  37.9 0.7 copy.63
  38.6 2.4 %collective-permute-start.3 = (bf16[512,256]{1,0:T(8,128)(2,1)S(1)}, bf16[512,256]{1,0:T(8,128)(2,1)S(1)}, u32[]{:S(2)}, u32[]{:S(2)}) collective-permute-start(bf16[512,256]{1,0:T(8,128)(2,1)S(1)} %bitcast.62), channel_id=1, source_target_pairs={{1,0},{2,1},{3,2},{4,3},{5,4},{6,5},{7,6},{8,7},{9,8},{10,9},{11,1... | collective-permute-start | bytes 786440 | tf_op jit(solution)/shard_map/ppermute | solution.py:14
  41.0 4.6 %collective-permute-start.2 = (bf16[512,256]{1,0:T(8,128)(2,1)S(1)}, bf16[512,256]{1,0:T(8,128)(2,1)S(1)}, u32[]{:S(2)}, u32[]{:S(2)}) collective-permute-start(bf16[512,256]{1,0:T(8,128)(2,1)S(1)} %bitcast.63), channel_id=1, source_target_pairs={{0,1},{1,2},{2,3},{3,4},{4,5},{5,6},{6,7},{7,8},{8,9},{9,10},{10,1... | collective-permute-start | bytes 786440 | tf_op jit(solution)/shard_map/ppermute | solution.py:14
  45.7 5.3 %all-to-all-start.1 = ((bf16[64,8,256]{2,0,1:T(8,128)(2,1)}), bf16[64,8,256]{2,0,1:T(8,128)(2,1)S(1)}, u32[]{:S(2)}, u32[]{:S(2)}) async-start(bf16[64,8,256]{2,0,1:T(8,128)(2,1)} %bitcast.46), calls=%async_computation.1 | async-start | bytes 524288 | tf_op jit(solution)/shard_map/all_to_all | solution.py:32
  51.0 0.1 copy.47
  51.1 0.1 copy.48
  51.3 0.0 collective-permute-done.1
  51.3 0.1 pad_maximum_fusion
  51.4 5.8 %all-to-all-done.1 = bf16[64,8,256]{2,0,1:T(8,128)(2,1)S(1)} async-done(((bf16[64,8,256]{2,0,1:T(8,128)(2,1)}), bf16[64,8,256]{2,0,1:T(8,128)(2,1)S(1)}, u32[]{:S(2)}, u32[]{:S(2)}) %all-to-all-start.1) | async-done | bytes 262176 | tf_op jit(solution)/shard_map/all_to_all | solution.py:32
  57.1 0.6 fusion.45
  57.7 0.5 exponential_reduce_fusion
  58.2 1.6 %fusion.21 = f32[1536,128]{0,1:T(8,128)} fusion(f32[1536,512]{1,0:T(8,128)S(1)} %get-tuple-element.11, f32[512]{0:T(512)S(1)} %log_add_fusion, bf16[512,256]{1,0:T(8,128)(2,1)S(1)} %bitcast.49), kind=kOutput, calls=%fused_computation.44 | convolution fusion | flops 202899456 | bytes 4065280 | tf_op jit(solution)/shard_map/dot_general | solution.py:24
  59.8 0.0 collective-permute-done.3
  59.8 0.0 collective-permute-done.2
  59.8 0.1 pad_maximum_fusion.1
  59.9 0.6 multiply_reduce_fusion
  60.5 0.8 fusion.6
  61.3 1.1 convolution_convert_fusion
  62.4 1.6 %fusion.34 = f32[1536,128]{0,1:T(8,128)} fusion(bf16[1536,512]{1,0:T(8,128)(2,1)S(1)} %fusion.6, bf16[512,256]{1,0:T(8,128)(2,1)S(1)} %bitcast.54), kind=kOutput, calls=%fused_computation.62 | convolution fusion | flops 201326592 | bytes 2490368 | tf_op jit(solution)/shard_map/dot_general | solution.py:24
  64.0 1.6 %fusion.46 = (f32[512]{0:T(512)S(1)}, f32[1536,512]{1,0:T(8,128)S(1)}) fusion(bf16[512,256]{1,0:T(8,128)(2,1)} %bitcast.55, bf16[1536,256]{1,0:T(8,128)(2,1)} %copy-done.5, pred[1536]{0:T(1024)(128)(4,1)S(1)} %pad_add_fusion), kind=kOutput, calls=%fused_computation.77 | convolution fusion | flops 203685376 | bytes 3673600 | tf_op jit(solution)/shard_map/dot_general | solution.py:18
  65.6 0.5 exponential_reduce_fusion.1
  66.1 1.6 %fusion.24 = f32[1536,128]{0,1:T(8,128)} fusion(f32[1536,512]{1,0:T(8,128)S(1)} %get-tuple-element.13, f32[512]{0:T(512)S(1)} %log_add_fusion.1, bf16[512,256]{1,0:T(8,128)(2,1)S(1)} %bitcast.51), kind=kOutput, calls=%fused_computation.45 | convolution fusion | flops 202899456 | bytes 4065280 | tf_op jit(solution)/shard_map/dot_general | solution.py:24
  67.7 0.6 multiply_reduce_fusion.1
  68.3 0.7 pad_maximum_fusion.4
  69.0 1.8 %copy.36 = bf16[512,256]{1,0:T(8,128)(2,1)} copy(bf16[512,256]{0,1:T(8,128)(2,1)} %pad_maximum_fusion.4) | data formatting | bytes 524288 | tf_op jit(solution)/shard_map/concatenate | solution.py:80
  70.8 4.1 %all-to-all-start.3 = ((bf16[8,64,256]{2,1,0:T(8,128)(2,1)}), bf16[8,64,256]{2,1,0:T(8,128)(2,1)}, u32[]{:S(2)}, u32[]{:S(2)}) async-start(bf16[8,64,256]{2,1,0:T(8,128)(2,1)} %bitcast.58), calls=%async_computation.3 | async-start | bytes 524288 | tf_op jit(solution)/shard_map/all_to_all | solution.py:97
  74.9 0.0 copy-start.8
  74.9 1.9 %fusion.7 = bf16[1536,512]{1,0:T(8,128)(2,1)S(1)} fusion(f32[1536,512]{1,0:T(8,128)S(1)} %get-tuple-element.13, f32[512]{0:T(512)S(1)} %get-tuple-element.16, f32[512]{0:T(512)S(1)} %log_add_fusion.1, bf16[1536,256]{1,0:T(8,128)(2,1)} %copy-done, bf16[512,256]{1,0:T(8,128)(2,1)S(1)} %bitcast.52), kind=kOutput, calls=%fused_computation.15 | convolution fusion | flops 205258752 | bytes 5246976 | tf_op jit(solution)/shard_map/dot_general | solution.py:18
  76.8 0.6 fusion.37
  77.5 0.0 copy-start.10
  77.5 1.1 fusion.15
  78.6 1.9 %collective-permute-start.4 = (f32[512,256]{0,1:T(8,128)}, f32[512,256]{0,1:T(8,128)}, u32[]{:S(2)}, u32[]{:S(2)}) collective-permute-start(f32[512,256]{0,1:T(8,128)} %get-tuple-element.6), channel_id=1, source_target_pairs={{1,0},{2,1},{3,2},{4,3},{5,4},{6,5},{7,6},{8,7},{9,8},{10,9},{11,1... | collective-permute-start | bytes 1572872 | tf_op jit(solution)/shard_map/ppermute | solution.py:14
  80.5 5.3 %collective-permute-start.5 = (f32[512,256]{0,1:T(8,128)}, f32[512,256]{0,1:T(8,128)}, u32[]{:S(2)}, u32[]{:S(2)}) collective-permute-start(f32[512,256]{0,1:T(8,128)} %get-tuple-element.7), channel_id=1, source_target_pairs={{0,1},{1,2},{2,3},{3,4},{4,5},{5,6},{6,7},{7,8},{8,9},{9,10},{10,1... | collective-permute-start | bytes 1572872 | tf_op jit(solution)/shard_map/ppermute | solution.py:14
  85.8 1.1 fusion.10
  86.9 1.9 %collective-permute-start.6 = (f32[512,256]{0,1:T(8,128)}, f32[512,256]{0,1:T(8,128)}, u32[]{:S(2)}, u32[]{:S(2)}) collective-permute-start(f32[512,256]{0,1:T(8,128)} %get-tuple-element.4), channel_id=1, source_target_pairs={{1,0},{2,1},{3,2},{4,3},{5,4},{6,5},{7,6},{8,7},{9,8},{10,9},{11,1... | collective-permute-start | bytes 1572872 | tf_op jit(solution)/shard_map/ppermute | solution.py:14
  88.8 5.1 %collective-permute-start.7 = (f32[512,256]{0,1:T(8,128)}, f32[512,256]{0,1:T(8,128)}, u32[]{:S(2)}, u32[]{:S(2)}) collective-permute-start(f32[512,256]{0,1:T(8,128)} %get-tuple-element.5), channel_id=1, source_target_pairs={{0,1},{1,2},{2,3},{3,4},{4,5},{5,6},{6,7},{7,8},{8,9},{9,10},{10,1... | collective-permute-start | bytes 1572872 | tf_op jit(solution)/shard_map/ppermute | solution.py:14
  93.9 0.4 convolution_convert_fusion.1
  94.4 0.8 copy.41
  95.2 0.0 all-to-all-done.3
  95.2 5.0 %all-to-all-start.5 = ((bf16[8,64,256]{2,1,0:T(8,128)(2,1)}), bf16[8,64,256]{2,1,0:T(8,128)(2,1)S(1)}, u32[]{:S(2)}, u32[]{:S(2)}) async-start(bf16[8,64,256]{2,1,0:T(8,128)(2,1)} %bitcast.60), calls=%async_computation.5 | async-start | bytes 524288 | tf_op jit(solution)/shard_map/all_to_all | solution.py:98
  100.3 4.0 %collective-permute-done.5 = f32[512,256]{0,1:T(8,128)} collective-permute-done((f32[512,256]{0,1:T(8,128)}, f32[512,256]{0,1:T(8,128)}, u32[]{:S(2)}, u32[]{:S(2)}) %collective-permute-start.5) | collective-permute-done | bytes 524320 | tf_op jit(solution)/shard_map/ppermute | solution.py:14
  104.3 2.0 %fusion.19 = bf16[512,256]{0,1:T(8,128)(2,1)} fusion(f32[512,256]{0,1:T(8,128)} %collective-permute-done.5, f32[512,256]{0,1:T(8,128)} %collective-permute-done.4, f32[1536,128]{0,1:T(8,128)S(1)} %fusion.37, f32[1536,128]{0,1:T(8,128)S(1)} %copy-done.4), kind=kLoop, calls=%fused_computation.41 | loop fusion | flops 524288 | bytes 2883584 | tf_op jit(solution)/shard_map/convert_element_type | solution.py:90
  106.3 1.8 %copy.43 = bf16[512,256]{1,0:T(8,128)(2,1)} copy(bf16[512,256]{0,1:T(8,128)(2,1)} %fusion.19) | data formatting | bytes 524288 | tf_op jit(solution)/shard_map/convert_element_type | solution.py:90
  108.1 3.9 %all-to-all-done.5 = bf16[8,64,256]{2,1,0:T(8,128)(2,1)S(1)} async-done(((bf16[8,64,256]{2,1,0:T(8,128)(2,1)}), bf16[8,64,256]{2,1,0:T(8,128)(2,1)S(1)}, u32[]{:S(2)}, u32[]{:S(2)}) %all-to-all-start.5) | async-done | bytes 262176 | tf_op jit(solution)/shard_map/all_to_all | solution.py:98
  112.0 4.9 %all-to-all-start.6 = ((bf16[8,64,256]{2,1,0:T(8,128)(2,1)}), bf16[8,64,256]{2,1,0:T(8,128)(2,1)S(1)}, u32[]{:S(2)}, u32[]{:S(2)}) async-start(bf16[8,64,256]{2,1,0:T(8,128)(2,1)} %bitcast.16), calls=%async_computation.6 | async-start | bytes 524288 | tf_op jit(solution)/shard_map/all_to_all | solution.py:99
  116.9 1.3 fusion.14
  118.2 0.8 copy.45
  119.0 4.0 %all-to-all-done.6 = bf16[8,64,256]{2,1,0:T(8,128)(2,1)S(1)} async-done(((bf16[8,64,256]{2,1,0:T(8,128)(2,1)}), bf16[8,64,256]{2,1,0:T(8,128)(2,1)S(1)}, u32[]{:S(2)}, u32[]{:S(2)}) %all-to-all-start.6) | async-done | bytes 262176 | tf_op jit(solution)/shard_map/all_to_all | solution.py:99
  123.0 3.4 %all-to-all-start.7 = ((bf16[8,64,256]{2,1,0:T(8,128)(2,1)}), bf16[8,64,256]{2,1,0:T(8,128)(2,1)S(1)}, u32[]{:S(2)}, u32[]{:S(2)}) async-start(bf16[8,64,256]{2,1,0:T(8,128)(2,1)} %bitcast.18), calls=%async_computation.7 | async-start | bytes 524288 | tf_op jit(solution)/shard_map/all_to_all | solution.py:100
  126.4 1.7 %copy.53 = bf16[8,8,8,256]{3,2,0,1:T(8,128)(2,1)} copy(bf16[8,8,8,256]{3,2,1,0:T(8,128)(2,1)} %bitcast.28) | data formatting | bytes 524288 | tf_op jit(solution)/shard_map/all_to_all | solution.py:97
  128.1 0.7 copy.54
  128.8 0.7 copy.55
  129.5 3.0 %all-to-all-done.7 = bf16[8,64,256]{2,1,0:T(8,128)(2,1)S(1)} async-done(((bf16[8,64,256]{2,1,0:T(8,128)(2,1)}), bf16[8,64,256]{2,1,0:T(8,128)(2,1)S(1)}, u32[]{:S(2)}, u32[]{:S(2)}) %all-to-all-start.7) | async-done | bytes 262176 | tf_op jit(solution)/shard_map/all_to_all | solution.py:100
  132.5 0.7 copy.56
  (33 shorter events, 0.1 us)
Async XLA Ops:
  0.6 37.2 %copy-start.9 = (bf16[64,2048]{1,0:T(8,128)(2,1)S(1)}, bf16[64,2048]{1,0:T(8,128)(2,1)}, u32[]{:S(2)}) copy-start(bf16[64,2048]{1,0:T(8,128)(2,1)} %param.4) | copy-start | bytes 786436
  2.4 12.0 %all-to-all-start = ((bf16[64,8,256]{2,0,1:T(8,128)(2,1)}), bf16[64,8,256]{2,0,1:T(8,128)(2,1)S(1)}, u32[]{:S(2)}, u32[]{:S(2)}) async-start(bf16[64,8,256]{2,0,1:T(8,128)(2,1)} %bitcast.47), calls=%async_computation | async-start | bytes 524288 | tf_op jit(solution)/shard_map/all_to_all | solution.py:33
  14.4 9.5 %all-to-all-start.2 = ((bf16[64,8,256]{2,0,1:T(8,128)(2,1)}), bf16[64,8,256]{2,0,1:T(8,128)(2,1)S(1)}, u32[]{:S(2)}, u32[]{:S(2)}) async-start(bf16[64,8,256]{2,0,1:T(8,128)(2,1)} %bitcast.45), calls=%async_computation.2 | async-start | bytes 524288 | tf_op jit(solution)/shard_map/all_to_all | solution.py:34
  23.8 21.8 %all-to-all-start.4 = ((bf16[64,8,256]{2,0,1:T(8,128)(2,1)}), bf16[64,8,256]{2,0,1:T(8,128)(2,1)S(1)}, u32[]{:S(2)}, u32[]{:S(2)}) async-start(bf16[64,8,256]{2,0,1:T(8,128)(2,1)} %bitcast.44), calls=%async_computation.4 | async-start | bytes 524288 | tf_op jit(solution)/shard_map/all_to_all | solution.py:35
  27.3 24.0 %collective-permute-start.1 = (bf16[512,256]{1,0:T(8,128)(2,1)S(1)}, bf16[512,256]{1,0:T(8,128)(2,1)S(1)}, u32[]{:S(2)}, u32[]{:S(2)}) collective-permute-start(bf16[512,256]{1,0:T(8,128)(2,1)S(1)} %bitcast.65), channel_id=1, source_target_pairs={{1,0},{2,1},{3,2},{4,3},{5,4},{6,5},{7,6},{8,7},{9,8},{10,9},{11,1... | collective-permute-start | bytes 786440 | tf_op jit(solution)/shard_map/ppermute | solution.py:14
  35.9 15.4 %collective-permute-start = (bf16[512,256]{1,0:T(8,128)(2,1)S(1)}, bf16[512,256]{1,0:T(8,128)(2,1)S(1)}, u32[]{:S(2)}, u32[]{:S(2)}) collective-permute-start(bf16[512,256]{1,0:T(8,128)(2,1)S(1)} %bitcast.66), channel_id=1, source_target_pairs={{0,1},{1,2},{2,3},{3,4},{4,5},{5,6},{6,7},{7,8},{8,9},{9,10},{10,1... | collective-permute-start | bytes 786440 | tf_op jit(solution)/shard_map/ppermute | solution.py:14
  38.6 21.2 %collective-permute-start.3 = (bf16[512,256]{1,0:T(8,128)(2,1)S(1)}, bf16[512,256]{1,0:T(8,128)(2,1)S(1)}, u32[]{:S(2)}, u32[]{:S(2)}) collective-permute-start(bf16[512,256]{1,0:T(8,128)(2,1)S(1)} %bitcast.62), channel_id=1, source_target_pairs={{1,0},{2,1},{3,2},{4,3},{5,4},{6,5},{7,6},{8,7},{9,8},{10,9},{11,1... | collective-permute-start | bytes 786440 | tf_op jit(solution)/shard_map/ppermute | solution.py:14
  41.0 18.8 %collective-permute-start.2 = (bf16[512,256]{1,0:T(8,128)(2,1)S(1)}, bf16[512,256]{1,0:T(8,128)(2,1)S(1)}, u32[]{:S(2)}, u32[]{:S(2)}) collective-permute-start(bf16[512,256]{1,0:T(8,128)(2,1)S(1)} %bitcast.63), channel_id=1, source_target_pairs={{0,1},{1,2},{2,3},{3,4},{4,5},{5,6},{6,7},{7,8},{8,9},{9,10},{10,1... | collective-permute-start | bytes 786440 | tf_op jit(solution)/shard_map/ppermute | solution.py:14
  45.7 11.5 %all-to-all-start.1 = ((bf16[64,8,256]{2,0,1:T(8,128)(2,1)}), bf16[64,8,256]{2,0,1:T(8,128)(2,1)S(1)}, u32[]{:S(2)}, u32[]{:S(2)}) async-start(bf16[64,8,256]{2,0,1:T(8,128)(2,1)} %bitcast.46), calls=%async_computation.1 | async-start | bytes 524288 | tf_op jit(solution)/shard_map/all_to_all | solution.py:32
  51.3 10.0 %copy-start.5 = (bf16[1536,256]{1,0:T(8,128)(2,1)}, bf16[1536,256]{1,0:T(8,128)(2,1)S(1)}, u32[]{:S(2)}) copy-start(bf16[1536,256]{1,0:T(8,128)(2,1)S(1)} %pad_maximum_fusion) | copy-start | bytes 2359300
  57.1 5.3 %copy-start.7 = (bf16[64,8,256]{2,0,1:T(8,128)(2,1)}, bf16[64,8,256]{2,0,1:T(8,128)(2,1)S(1)}, u32[]{:S(2)}) copy-start(bf16[64,8,256]{2,0,1:T(8,128)(2,1)S(1)} %all-to-all-done.1) | copy-start | bytes 786436
  59.9 7.8 %copy-start = (bf16[1536,256]{1,0:T(8,128)(2,1)}, bf16[1536,256]{1,0:T(8,128)(2,1)S(1)}, u32[]{:S(2)}) copy-start(bf16[1536,256]{1,0:T(8,128)(2,1)S(1)} %pad_maximum_fusion.1) | copy-start | bytes 2359300
  70.8 24.4 %all-to-all-start.3 = ((bf16[8,64,256]{2,1,0:T(8,128)(2,1)}), bf16[8,64,256]{2,1,0:T(8,128)(2,1)}, u32[]{:S(2)}, u32[]{:S(2)}) async-start(bf16[8,64,256]{2,1,0:T(8,128)(2,1)} %bitcast.58), calls=%async_computation.3 | async-start | bytes 524288 | tf_op jit(solution)/shard_map/all_to_all | solution.py:97
  74.9 1.9 %copy-start.8 = (bf16[64,8,256]{2,0,1:T(8,128)(2,1)S(1)}, bf16[64,8,256]{2,0,1:T(8,128)(2,1)}, u32[]{:S(2)}) copy-start(bf16[64,8,256]{2,0,1:T(8,128)(2,1)} %copy-done.7) | copy-start | bytes 786436
  74.9 2.6 %copy-start.3 = (f32[1536,128]{0,1:T(8,128)S(1)}, f32[1536,128]{0,1:T(8,128)}, u32[]{:S(2)}) copy-start(f32[1536,128]{0,1:T(8,128)} %fusion.34) | copy-start | bytes 2359300
  76.8 9.0 %copy-start.1 = (f32[1536,128]{0,1:T(8,128)S(1)}, f32[1536,128]{0,1:T(8,128)}, u32[]{:S(2)}) copy-start(f32[1536,128]{0,1:T(8,128)} %fusion.21) | copy-start | bytes 2359300
  76.8 9.0 %copy-start.2 = (f32[1536,128]{0,1:T(8,128)S(1)}, f32[1536,128]{0,1:T(8,128)}, u32[]{:S(2)}) copy-start(f32[1536,128]{0,1:T(8,128)} %fusion.24) | copy-start | bytes 2359300
  77.5 16.5 %copy-start.6 = (bf16[1536,256]{1,0:T(8,128)(2,1)S(1)}, bf16[1536,256]{1,0:T(8,128)(2,1)}, u32[]{:S(2)}) copy-start(bf16[1536,256]{1,0:T(8,128)(2,1)} %copy-done.5) | copy-start | bytes 2359300
  77.5 16.9 %copy-start.10 = (bf16[512,128]{0,1:T(8,128)(2,1)S(1)}, bf16[512,128]{0,1:T(8,128)(2,1)}, u32[]{:S(2)}) copy-start(bf16[512,128]{0,1:T(8,128)(2,1)} %convolution_convert_fusion) | copy-start | bytes 393220
  78.6 21.7 %collective-permute-start.4 = (f32[512,256]{0,1:T(8,128)}, f32[512,256]{0,1:T(8,128)}, u32[]{:S(2)}, u32[]{:S(2)}) collective-permute-start(f32[512,256]{0,1:T(8,128)} %get-tuple-element.6), channel_id=1, source_target_pairs={{1,0},{2,1},{3,2},{4,3},{5,4},{6,5},{7,6},{8,7},{9,8},{10,9},{11,1... | collective-permute-start | bytes 1572872 | tf_op jit(solution)/shard_map/ppermute | solution.py:14
  80.5 23.8 %copy-start.4 = (f32[1536,128]{0,1:T(8,128)S(1)}, f32[1536,128]{0,1:T(8,128)}, u32[]{:S(2)}) copy-start(f32[1536,128]{0,1:T(8,128)} %fusion.34) | copy-start | bytes 2359300
  80.5 23.8 %collective-permute-start.5 = (f32[512,256]{0,1:T(8,128)}, f32[512,256]{0,1:T(8,128)}, u32[]{:S(2)}, u32[]{:S(2)}) collective-permute-start(f32[512,256]{0,1:T(8,128)} %get-tuple-element.7), channel_id=1, source_target_pairs={{0,1},{1,2},{2,3},{3,4},{4,5},{5,6},{6,7},{7,8},{8,9},{9,10},{10,1... | collective-permute-start | bytes 1572872 | tf_op jit(solution)/shard_map/ppermute | solution.py:14
  86.9 30.0 %collective-permute-start.6 = (f32[512,256]{0,1:T(8,128)}, f32[512,256]{0,1:T(8,128)}, u32[]{:S(2)}, u32[]{:S(2)}) collective-permute-start(f32[512,256]{0,1:T(8,128)} %get-tuple-element.4), channel_id=1, source_target_pairs={{1,0},{2,1},{3,2},{4,3},{5,4},{6,5},{7,6},{8,7},{9,8},{10,9},{11,1... | collective-permute-start | bytes 1572872 | tf_op jit(solution)/shard_map/ppermute | solution.py:14
  88.8 28.1 %collective-permute-start.7 = (f32[512,256]{0,1:T(8,128)}, f32[512,256]{0,1:T(8,128)}, u32[]{:S(2)}, u32[]{:S(2)}) collective-permute-start(f32[512,256]{0,1:T(8,128)} %get-tuple-element.5), channel_id=1, source_target_pairs={{0,1},{1,2},{2,3},{3,4},{4,5},{5,6},{6,7},{7,8},{8,9},{9,10},{10,1... | collective-permute-start | bytes 1572872 | tf_op jit(solution)/shard_map/ppermute | solution.py:14
  95.2 16.7 %all-to-all-start.5 = ((bf16[8,64,256]{2,1,0:T(8,128)(2,1)}), bf16[8,64,256]{2,1,0:T(8,128)(2,1)S(1)}, u32[]{:S(2)}, u32[]{:S(2)}) async-start(bf16[8,64,256]{2,1,0:T(8,128)(2,1)} %bitcast.60), calls=%async_computation.5 | async-start | bytes 524288 | tf_op jit(solution)/shard_map/all_to_all | solution.py:98
  112.0 11.0 %all-to-all-start.6 = ((bf16[8,64,256]{2,1,0:T(8,128)(2,1)}), bf16[8,64,256]{2,1,0:T(8,128)(2,1)S(1)}, u32[]{:S(2)}, u32[]{:S(2)}) async-start(bf16[8,64,256]{2,1,0:T(8,128)(2,1)} %bitcast.16), calls=%async_computation.6 | async-start | bytes 524288 | tf_op jit(solution)/shard_map/all_to_all | solution.py:99
  123.0 9.5 %all-to-all-start.7 = ((bf16[8,64,256]{2,1,0:T(8,128)(2,1)}), bf16[8,64,256]{2,1,0:T(8,128)(2,1)S(1)}, u32[]{:S(2)}, u32[]{:S(2)}) async-start(bf16[8,64,256]{2,1,0:T(8,128)(2,1)} %bitcast.18), calls=%async_computation.7 | async-start | bytes 524288 | tf_op jit(solution)/shard_map/all_to_all | solution.py:100
where the time goes:
time: 135 us; the launch traced here: 133 us
  starting transfers between devices  67.2 us (50%)
  waiting for transfers between devices  29.5 us (22%)
  local copies, waits for them, and re-layouts  15.2 us (11%)
  matrix products  13 us (10%)
  other arithmetic  7.34 us (5%)
    ppermute x8, starting transfers between devices, passed_along(): return lax.ppermute(value, axis, pairs)  31.8 us
    all_to_all x1, starting transfers between devices, on_device(): lax.all_to_all(key_rows, 'head', split_axis=1, concat_axis=0, tiled=True)  5.86 us
    all_to_all x1, waiting for transfers between devices, on_device(): lax.all_to_all(query_rows, 'head', split_axis=1, concat_axis=0, tiled=True)  5.78 us
    dot_general x4, matrix products, transposed_times(): lax.dot_general(lhs_matrix, rhs_matrix, (((0,), (0,)), ((), ())), preferr...  5.37 us
    all_to_all x1, starting transfers between devices, on_device(): lax.all_to_all(query_rows, 'head', split_axis=1, concat_axis=0, tiled=True)  5.35 us
    all_to_all x1, starting transfers between devices, on_device(): lax.all_to_all(grad_query, 'head', split_axis=0, concat_axis=1, tiled=True)  5.03 us
    dot_general x4, matrix products, times_transposed(): lax.dot_general(lhs_matrix, rhs_matrix, (((1,), (1,)), ((), ())), preferr...  4.88 us
    all_to_all x1, starting transfers between devices, on_device(): lax.all_to_all(grad_key, 'head', split_axis=0, concat_axis=1, tiled=True)  4.85 us
  transfers between devices with their start and end apart: 16, of which 7 were waited for; matrix products, arithmetic and copies ran while one was open for 17% of the time, Pallas kernels for 0%

commit v1 on v0

v1 whole, which is shorter than its diff:
```python
import math

import jax
import jax.numpy as jnp
from jax import lax
from jax.experimental import pallas as pl
from jax.experimental.pallas import tpu as pltpu
from jax.sharding import PartitionSpec as P

DH = 128
WIDE = 2 * DH
SEG = 512
ROWS = 64
Q_ROWS = 128
SCALE = 1.0 / math.sqrt(DH)
SCALE_2 = SCALE * math.log2(math.e)
BF16 = jnp.bfloat16
F32 = jnp.float32
MESH = pl.DeviceIdType.MESH
PEERS = ((0, 2), (1, 2), (1, 1), (0, 1), (1, 3), (0, 3), (1, 0))
PIECE = 128


def nt(lhs, rhs):
    return lax.dot_general(lhs, rhs, (((1,), (1,)), ((), ())), preferred_element_type=F32)


def nn(lhs, rhs):
    return lax.dot_general(lhs, rhs, (((1,), (0,)), ((), ())), preferred_element_type=F32)


def kernel(
    q_in, k_in, v_in, g_in, att_out, dq_out, dk_out, dv_out,
    kw, vw, q_s, g_s, e_s, d_s, gp_s, att_st, dq_st, dk_st, dv_st, own_k, own_v, t_send, t_recv,
    in_send, in_recv, halo_send, halo_recv, term_send, term_recv, out_send, out_recv,
):
    head = lax.axis_index("head")
    blk = lax.axis_index("blk")
    count = lax.axis_size("blk")
    y_hi = (blk // 2) % 2
    core = blk % 2
    mine = (head + 4 * y_hi) % 8
    peers = [((head // 4 + dy) % 2) * 4 + (head % 4 + dx) % 4 for dy, dx in PEERS]
    across = (head + 4) % 8
    up = {"blk": (blk + 1) % count, "head": core * across + (1 - core) * head}
    down = {"blk": (blk + count - 1) % count, "head": core * head + (1 - core) * across}
    has_lower = blk > 0
    has_upper = blk < count - 1

    def remote(src, dst, send, recv, target):
        copy = pltpu.make_async_remote_copy(
            src_ref=src, dst_ref=dst, send_sem=send, recv_sem=recv, device_id=target, device_id_type=MESH
        )
        copy.start()

    def settle(ref, sem):
        pltpu.make_async_copy(ref, ref, sem).wait()

    barrier = pltpu.get_barrier_semaphore()
    for target in [{"head": p} for p in peers] + [up, down]:
        pl.semaphore_signal(barrier, inc=1, device_id=target, device_id_type=MESH)
    pl.semaphore_wait(barrier, len(peers) + 2)

    my_rows = pl.ds(pl.multiple_of(head * ROWS, ROWS), ROWS)

    def spread(src, landing, start, width, send, recv):
        for p in peers:
            column = pl.multiple_of(((p + 4 * y_hi) % 8) * WIDE + start, DH)
            remote(src.at[:, pl.ds(column, width)], landing, send, recv, {"head": p})
        column = pl.multiple_of(mine * WIDE + start, DH)
        pltpu.make_async_copy(src.at[:, pl.ds(column, width)], landing, recv).start()

    spread(k_in, kw.at[1, my_rows, :], 0, WIDE, in_send.at[0], in_recv.at[0])
    spread(v_in, vw.at[1, my_rows, :], 0, WIDE, in_send.at[1], in_recv.at[1])
    for hd in range(2):
        spread(q_in, q_s.at[hd, my_rows, :], hd * DH, DH, in_send.at[2 + 2 * hd], in_recv.at[2 + 2 * hd])
        spread(g_in, g_s.at[hd, my_rows, :], hd * DH, DH, in_send.at[3 + 2 * hd], in_recv.at[3 + 2 * hd])

    for n, window in enumerate((kw, vw)):
        settle(window.at[1], in_recv.at[n])
        for hd in range(2):
            cols = pl.ds(hd * DH, DH)
            for r in range(0, SEG, PIECE):
                rows = pl.ds(r, PIECE)
                remote(window.at[1, rows, cols], window.at[0, rows, cols],
                       halo_send.at[n, hd, 0], halo_recv.at[n, hd, 0], up)
                remote(window.at[1, rows, cols], window.at[2, rows, cols],
                       halo_send.at[n, hd, 1], halo_recv.at[n, hd, 1], down)

    factors = [jnp.where(has_lower, SCALE_2, 0.0), SCALE_2, jnp.where(has_upper, SCALE_2, 0.0)]

    def collect(staged, out, n, hd):
        for p in peers:
            rows = pl.ds(pl.multiple_of(p * ROWS, ROWS), ROWS)
            column = pl.multiple_of(mine * WIDE + hd * DH, DH)
            remote(staged.at[hd, rows, :], out.at[:, pl.ds(column, DH)],
                   out_send.at[n, hd], out_recv.at[n], {"head": p})
        column = pl.multiple_of(mine * WIDE + hd * DH, DH)
        pltpu.make_async_copy(staged.at[hd, my_rows, :], out.at[:, pl.ds(column, DH)], out_recv.at[n]).start()

    def attend(hd):
        cols = pl.ds(hd * DH, DH)
        for r in range(0, SEG, Q_ROWS):
            rows = pl.ds(r, Q_ROWS)
            query = q_s[hd, rows, :]
            scores = [nt(query, kw[j, :, cols]) for j in range(3)]
            tops = [jnp.max(s, axis=1, keepdims=True) for s in scores]
            top = jnp.maximum(
                jnp.maximum(jnp.where(has_lower, tops[0], -jnp.inf), tops[1]),
                jnp.where(has_upper, tops[2], -jnp.inf),
            ) * SCALE_2
            shifts = [jnp.where(has_lower, top, 1e30), top, jnp.where(has_upper, top, 1e30)]
            total = 0.0
            attended = 0.0
            for j in range(3):
                e = jnp.exp2(scores[j] * factors[j] - shifts[j])
                total = total + jnp.sum(e, axis=1, keepdims=True)
                low = e.astype(BF16)
                e_s[j, rows, :] = low
                attended = attended + nn(low, vw[j, :, cols])
            inverse = 1.0 / total
            attended = attended * inverse
            att_st[hd, rows, :] = attended.astype(BF16)
            scaled = (g_s[hd, rows, :].astype(F32) * (inverse * SCALE)).astype(BF16)
            gp_s[rows, :] = scaled
            delta = jnp.sum(scaled.astype(F32) * attended, axis=1, keepdims=True)
            for j in range(3):
                dprobs = nt(scaled, vw[j, :, cols])
                d_s[j, rows, :] = (dprobs - delta).astype(BF16) * e_s[j, rows, :]

    def send_term(n, hd, side):
        target = down if side == 0 else up
        for r in range(0, SEG, PIECE):
            rows = pl.ds(r, PIECE)
            remote(t_send.at[n, hd, side, rows, :], t_recv.at[n, hd, 1 - side, rows, :],
                   term_send.at[n, hd, side], term_recv.at[n, hd, 1 - side], target)

    def backward(hd):
        cols = pl.ds(hd * DH, DH)
        grads_t = gp_s[...].T
        queries_t = q_s[hd].T
        for side in range(2):
            t_send[1, hd, side] = (nn(grads_t, e_s[2 * side]) * (1.0 / SCALE)).T.astype(BF16)
            send_term(1, hd, side)
        for side in range(2):
            t_send[0, hd, side] = nn(queries_t, d_s[2 * side]).T.astype(BF16)
            send_term(0, hd, side)
        own_v[hd] = (nn(grads_t, e_s[1]) * (1.0 / SCALE)).T
        own_k[hd] = nn(queries_t, d_s[1]).T
        for r in range(0, SEG, Q_ROWS):
            rows = pl.ds(r, Q_ROWS)
            dq_st[hd, rows, :] = (
                nn(d_s[0, rows, :], kw[0, :, cols]) + nn(d_s[1, rows, :], kw[1, :, cols])
                + nn(d_s[2, rows, :], kw[2, :, cols])
            ).astype(BF16)

    def finish(hd):
        for n, own, staged, out in ((1, own_v, dv_st, dv_out), (0, own_k, dk_st, dk_out)):
            for side in range(2):
                settle(t_recv.at[n, hd, side], term_recv.at[n, hd, side])
            staged[hd] = (
                own[hd] + t_recv[n, hd, 0].astype(F32) + t_recv[n, hd, 1].astype(F32)
            ).astype(BF16)
            collect(staged, out, 2 + n, hd)

    for hd in range(2):
        cols = pl.ds(hd * DH, DH)
        settle(q_s.at[hd], in_recv.at[2 + 2 * hd])
        settle(g_s.at[hd], in_recv.at[3 + 2 * hd])
        for n, window in enumerate((kw, vw)):
            settle(window.at[0, :, cols], halo_recv.at[n, hd, 0])
            settle(window.at[2, :, cols], halo_recv.at[n, hd, 1])
        attend(hd)
        collect(att_st, att_out, 0, hd)
        if hd == 1:
            finish(0)
        backward(hd)
        collect(dq_st, dq_out, 1, hd)
    finish(1)

    for n, out in enumerate((att_out, dq_out, dk_out, dv_out)):
        settle(out, out_recv.at[n])
    seven = pl.ds(0, 7 * ROWS)
    settle(kw.at[1, seven, :], in_send.at[0])
    settle(vw.at[1, seven, :], in_send.at[1])
    for hd in range(2):
        cols = pl.ds(hd * DH, DH)
        settle(q_s.at[hd, seven, :], in_send.at[2 + 2 * hd])
        settle(g_s.at[hd, seven, :], in_send.at[3 + 2 * hd])
        for n, window in enumerate((kw, vw)):
            for side in range(2):
                settle(window.at[1, :, cols], halo_send.at[n, hd, side])
                settle(t_send.at[n, hd, side], term_send.at[n, hd, side])
        for n, staged in enumerate((att_st, dq_st, dk_st, dv_st)):
            settle(staged.at[hd, seven, :], out_send.at[n, hd])


def on_device(query_rows, key_rows, value_rows, grad_out):
    dma = pltpu.SemaphoreType.DMA
    seg_half = pltpu.VMEM((2, SEG, DH), BF16)
    seg_full = pltpu.VMEM((2, SEG, DH), F32)
    out = jax.ShapeDtypeStruct(query_rows.shape, BF16)
    return pl.pallas_call(
        kernel,
        out_shape=[out] * 4,
        in_specs=[pl.BlockSpec(memory_space=pltpu.HBM)] * 4,
        out_specs=[pl.BlockSpec(memory_space=pltpu.HBM)] * 4,
        scratch_shapes=[
            pltpu.VMEM((3, SEG, WIDE), BF16),
            pltpu.VMEM((3, SEG, WIDE), BF16),
            seg_half,
            seg_half,
            pltpu.VMEM((3, SEG, SEG), BF16),
            pltpu.VMEM((3, SEG, SEG), BF16),
            pltpu.VMEM((SEG, DH), BF16),
            seg_half,
            seg_half,
            seg_half,
            seg_half,
            seg_full,
            seg_full,
            pltpu.VMEM((2, 2, 2, SEG, DH), BF16),
            pltpu.VMEM((2, 2, 2, SEG, DH), BF16),
            dma((6,)),
            dma((6,)),
            dma((2, 2, 2)),
            dma((2, 2, 2)),
            dma((2, 2, 2)),
            dma((2, 2, 2)),
            dma((4, 2)),
            dma((4,)),
        ],
        compiler_params=pltpu.CompilerParams(
            collective_id=0, has_side_effects=True, vmem_limit_bytes=63 * 2**20
        ),
        cost_estimate=pl.CostEstimate(flops=2_400_000_000, bytes_accessed=2 * 2**20, transcendentals=1_600_000),
        name="window_attention",
    )(query_rows, key_rows, value_rows, grad_out)


def solution(mesh):
    spec = P(("blk", "head"), None)
    return jax.shard_map(
        on_device, mesh=mesh, in_specs=(spec,) * 4, out_specs=(spec,) * 4, check_vma=False
    )
```

time: 135 us -> 52.2 us (0.39)
  the two profiles are of different devices: /device:TPU:1 before, /device:TPU:8 now
where the time goes in v1:
time: 52.2 us; the launch traced here: 52 us
  Pallas kernels  46.9 us (90%)
  local copies, waits for them, and re-layouts  4.5 us (9%)
  between operations  0.65 us (1%)
    pallas_call x1, Pallas kernels, on_device(): pl.pallas_call(kernel, out_shape=[out] * 4, in_specs=[pl.BlockSpec(memory...  46.9 us
    unnamed x10, local copies, waits for them, and re-layouts  4.5 us

profile of v1, /device:TPU:8, one launch (start us, length us, event | category | flops | bytes accessed | tf_op | source)
XLA Modules:
  0.0 52.0 jit_solution(9571322928078623799)
XLA Ops:
  0.6 46.9 %window_attention.1 = (bf16[64,2048]{1,0:T(8,128)(2,1)}, bf16[64,2048]{1,0:T(8,128)(2,1)}, bf16[64,2048]{1,0:T(8,128)(2,1)}, bf16[64,2048]{1,0:T(8,128)(2,1)}) custom-call(bf16[64,2048]{1,0:T(8,128)(2,1)} %q_in.1, bf16[64,2048]{1,0:T(8,128)(2,1)} %k_in.1, bf16[64,2048]{1,0:T(8,128)(2,1)} %v_in.1, bf16[64,2048]{1,0:T(8,128)(2,1)} %g_in.1), custom_call_target="tpu_custom_call" | custom-call | flops 2400000000 | bytes 2097152 | tf_op jit(solution)/shard_map/window_attention/pallas_call | solution.py:203
  47.5 0.0 copy-start.2
  47.5 1.7 %copy.12 = bf16[64,2048]{1,0:T(8,128)(2,1)} copy(bf16[64,2048]{1,0:T(8,128)(2,1)} %get-tuple-element.8) | data formatting | bytes 524288
  49.2 0.0 copy-done.2
  49.2 0.0 copy-start.1
  49.2 0.7 %copy.13 = bf16[64,2048]{1,0:T(8,128)(2,1)} copy(bf16[64,2048]{1,0:T(8,128)(2,1)S(1)} %copy-done.2) | data formatting | bytes 524288
  49.9 0.3 copy-done.1
  50.3 0.0 copy-start
  50.3 0.7 %copy.14 = bf16[64,2048]{1,0:T(8,128)(2,1)} copy(bf16[64,2048]{1,0:T(8,128)(2,1)S(1)} %copy-done.1) | data formatting | bytes 524288
  51.0 0.3 copy-done
  51.3 0.7 %copy.15 = bf16[64,2048]{1,0:T(8,128)(2,1)} copy(bf16[64,2048]{1,0:T(8,128)(2,1)S(1)} %copy-done) | data formatting | bytes 524288
Async XLA Ops:
  47.5 1.7 %copy-start.2 = (bf16[64,2048]{1,0:T(8,128)(2,1)S(1)}, bf16[64,2048]{1,0:T(8,128)(2,1)}, u32[]{:S(2)}) copy-start(bf16[64,2048]{1,0:T(8,128)(2,1)} %get-tuple-element.9) | copy-start | bytes 786436
  49.2 1.0 %copy-start.1 = (bf16[64,2048]{1,0:T(8,128)(2,1)S(1)}, bf16[64,2048]{1,0:T(8,128)(2,1)}, u32[]{:S(2)}) copy-start(bf16[64,2048]{1,0:T(8,128)(2,1)} %get-tuple-element.10) | copy-start | bytes 786436
  50.3 1.0 %copy-start = (bf16[64,2048]{1,0:T(8,128)(2,1)S(1)}, bf16[64,2048]{1,0:T(8,128)(2,1)}, u32[]{:S(2)}) copy-start(bf16[64,2048]{1,0:T(8,128)(2,1)} %get-tuple-element.11) | copy-start | bytes 786436

commit v2 on v1

v2 whole, which is shorter than its diff:
```python
import math

import jax
import jax.numpy as jnp
from jax import lax
from jax.experimental import pallas as pl
from jax.experimental.pallas import tpu as pltpu
from jax.sharding import PartitionSpec as P

DH = 128
HEADS = 16
SEG = 512
ROWS = 64
Q_ROWS = 128
SCALE = 1.0 / math.sqrt(DH)
SCALE_2 = SCALE * math.log2(math.e)
BF16 = jnp.bfloat16
F32 = jnp.float32
MESH = pl.DeviceIdType.MESH
PLANE = (
    (2, 2), (2, 1), (1, 2), (2, 3), (3, 2), (1, 1), (3, 3), (1, 3), (3, 1),
    (0, 2), (2, 0), (0, 1), (1, 0), (0, 3), (3, 0), (0, 0),
)
OWNERS = ((1, 2), (0, 2), (1, 1), (1, 3), (0, 1), (0, 3), (1, 0), (0, 0))


def nt(lhs, rhs):
    return lax.dot_general(lhs, rhs, (((1,), (1,)), ((), ())), preferred_element_type=F32)


def nn(lhs, rhs):
    return lax.dot_general(lhs, rhs, (((1,), (0,)), ((), ())), preferred_element_type=F32)


def kernel(
    q_in, k_in, v_in, g_in, att_out, dq_out, dk_out, dv_out,
    staged_in, landed, kw, vw, q_s, g_s, e_s, d_s, gp_s, att_f, inv_s, att_st, dq_st, dk_st, dv_st,
    t_send, t_recv, stage_sem, store_sem,
    in_send, in_recv, halo_send, halo_recv, term_send, term_recv, out_send, out_recv,
):
    head = lax.axis_index("head")
    blk = lax.axis_index("blk")
    planes = lax.axis_size("blk") // 4
    z, y_hi, core = blk // 4, (blk // 2) % 2, blk % 2
    y_lo, x = head // 4, head % 4
    y = 2 * y_hi + y_lo
    mine = 4 * y + x
    away = (y_hi + core) % 2
    at_home = away == 0
    at_end = jnp.where(z + core == 0, 1, 0) + jnp.where(z + core == planes, 1, 0)
    has_far = at_end == 0
    far = {"blk": blk - 3 + 6 * core, "head": head}
    near = {"blk": blk + 1 - 2 * core, "head": head}
    segs = (core, 1 - core)

    def remote(src, dst, send, recv, target):
        pltpu.make_async_remote_copy(
            src_ref=src, dst_ref=dst, send_sem=send, recv_sem=recv, device_id=target, device_id_type=MESH
        ).start()

    def settle(ref, sem):
        pltpu.make_async_copy(ref, ref, sem).wait()

    def owners(turn):
        for dy, dx in OWNERS:
            there = ((y_lo + dy) % 2) * 4 + (x + dx) % 4
            yield {"blk": 4 * z + 2 * core + segs[turn], "head": there}, there, turn == 0 and (dy, dx) == (0, 0)

    inputs = (k_in, v_in, q_in, g_in)
    staging = [pltpu.make_async_copy(src, staged_in.at[n], stage_sem.at[n]) for n, src in enumerate(inputs)]
    for copy in staging:
        copy.start()
    barrier = pltpu.get_barrier_semaphore()

    def greet(target):
        pl.semaphore_signal(barrier, inc=1, device_id=target, device_id_type=MESH)

    pl.when(has_far)(lambda: greet(far))
    greet(near)
    for turn in range(2):
        for target, _, own in owners(turn):
            if own:
                pl.when(jnp.logical_not(at_home))(lambda target=target: greet(target))
            else:
                greet(target)

    @pl.when(jnp.logical_not(has_far))
    def _():
        kw[3 * core] = jnp.zeros((SEG, DH), BF16)
        vw[3 * core] = jnp.zeros((SEG, DH), BF16)
        t_recv[0, 0] = jnp.zeros((SEG, DH), BF16)
        t_recv[1, 0] = jnp.zeros((SEG, DH), BF16)

    pl.semaphore_wait(barrier, 17 + away - at_end)

    my_rows = pl.ds(pl.multiple_of(head * ROWS, ROWS), ROWS)
    my_column = pl.ds(pl.multiple_of(mine * DH, DH), DH)

    def spread(n, landing):
        send, recv = in_send.at[n], in_recv.at[n, away]
        staging[n].wait()
        for dy, dx in PLANE:
            there_y, there_x = (y + dy) % 4, (x + dx) % 4
            columns = pl.ds(pl.multiple_of((4 * there_y + there_x) * DH, DH), DH)
            target = {"blk": 4 * z + 2 * (there_y // 2) + y_hi, "head": (there_y % 2) * 4 + there_x}

            def go(columns=columns, target=target):
                remote(staged_in.at[n, :, columns], landing, send, recv, target)

            if (dy, dx) == (0, 0):
                pl.when(jnp.logical_not(at_home))(go)

                @pl.when(at_home)
                def _():
                    pltpu.make_async_copy(inputs[n].at[:, my_column], landing, recv).start()
            else:
                go()

    spread(0, kw.at[1 + core, my_rows, :])
    spread(1, vw.at[1 + core, my_rows, :])
    spread(2, q_s.at[away, my_rows, :])
    spread(3, g_s.at[away, my_rows, :])

    for n, window in enumerate((kw, vw)):
        settle(window.at[1 + core], in_recv.at[n, 0])
        pl.when(has_far)(lambda n=n, window=window: remote(
            window.at[1 + core], window.at[3 - 3 * core], halo_send.at[n, 0], halo_recv.at[n, 0], far
        ))
        settle(window.at[2 - core], in_recv.at[n, 1])
        remote(window.at[2 - core], window.at[3 * core], halo_send.at[n, 1], halo_recv.at[n, 1], near)

    def collect(staged, n, turn):
        for target, there, own in owners(turn):
            rows = pl.ds(pl.multiple_of(there * ROWS, ROWS), ROWS)

            def go(rows=rows, target=target):
                remote(staged.at[turn, rows, :], landed.at[n, :, my_column], out_send.at[n], out_recv.at[n], target)

            if own:
                pl.when(jnp.logical_not(at_home))(go)

                @pl.when(at_home)
                def _():
                    landed[n, :, my_column] = staged[turn, my_rows, :]
            else:
                go()

    def attend(turn):
        seg = segs[turn]
        inside = (True, True, True)
        if turn == 0:
            inside = (core + (1 - at_end) > 0, True, 1 - core + (1 - at_end) > 0)
        factors = [SCALE_2 if ok is True else jnp.where(ok, SCALE_2, 0.0) for ok in inside]
        for r in range(0, SEG, Q_ROWS):
            rows = pl.ds(r, Q_ROWS)
            query = q_s[turn, rows, :]
            scores = [nt(query, kw[seg + j]) for j in range(3)]
            tops = [jnp.max(s, axis=1, keepdims=True) for s in scores]
            tops = [t if ok is True else jnp.where(ok, t, -jnp.inf) for t, ok in zip(tops, inside)]
            top = jnp.maximum(jnp.maximum(tops[0], tops[1]), tops[2]) * SCALE_2
            total = 0.0
            attended = 0.0
            for j in range(3):
                shift = top if inside[j] is True else jnp.where(inside[j], top, 1e30)
                e = jnp.exp2(scores[j] * factors[j] - shift)
                total = total + jnp.sum(e, axis=1, keepdims=True)
                low = e.astype(BF16)
                e_s[turn, j, rows, :] = low
                attended = attended + nn(low, vw[seg + j])
            inverse = 1.0 / total
            attended = attended * inverse
            att_st[turn, rows, :] = attended.astype(BF16)
            att_f[turn, rows, :] = attended
            inv_s[turn, rows, :] = inverse * SCALE

    def score_grads(turn):
        seg = segs[turn]
        for r in range(0, SEG, Q_ROWS):
            rows = pl.ds(r, Q_ROWS)
            scaled = (g_s[turn, rows, :].astype(F32) * inv_s[turn, rows, :]).astype(BF16)
            gp_s[turn, rows, :] = scaled
            delta = jnp.sum(scaled.astype(F32) * att_f[turn, rows, :], axis=1, keepdims=True)
            for j in range(3):
                dprobs = nt(scaled, vw[seg + j])
                d_s[turn, j, rows, :] = (dprobs - delta).astype(BF16) * e_s[turn, j, rows, :]

    def query_grads(turn):
        seg = segs[turn]
        for r in range(0, SEG, Q_ROWS):
            rows = pl.ds(r, Q_ROWS)
            dq_st[turn, rows, :] = sum(nn(d_s[turn, j, rows, :], kw[seg + j]) for j in range(3)).astype(BF16)

    def value_terms(pairs):
        return (sum(nn(gp_s[turn].T, e_s[turn, j]) for turn, j in pairs) * (1.0 / SCALE)).T

    def key_terms(pairs):
        return sum(nn(q_s[turn].T, d_s[turn, j]) for turn, j in pairs).T

    def send_terms(turn):
        outer = (2 * core, 2 - 2 * core)[turn]
        for n, terms in ((1, value_terms), (0, key_terms)):
            t_send[n, turn] = terms([(turn, outer)]).astype(BF16)

            def go(n=n):
                remote(t_send.at[n, turn], t_recv.at[n, turn], term_send.at[n, turn], term_recv.at[n, turn], (far, near)[turn])

            if turn == 0:
                pl.when(has_far)(go)
            else:
                go()

    def finish(turn):
        across = (2 * core, 2 - 2 * core)[turn]
        for n, terms, staged in ((1, value_terms, dv_st), (0, key_terms, dk_st)):
            own = terms([(turn, 1), (1 - turn, across)])

            def arrive(n=n):
                settle(t_recv.at[n, turn], term_recv.at[n, turn])

            if turn == 0:
                pl.when(has_far)(arrive)
            else:
                arrive()
            staged[turn] = (own + t_recv[n, turn].astype(F32)).astype(BF16)
            collect(staged, 2 + n, turn)

    for turn in (1, 0):
        settle(q_s.at[turn], in_recv.at[2, turn])
        for n, window in enumerate((kw, vw)):
            if turn == 0:
                pl.when(has_far)(lambda n=n, window=window: settle(window.at[3 * core], halo_recv.at[n, 0]))
            else:
                settle(window.at[3 - 3 * core], halo_recv.at[n, 1])
        attend(turn)
        collect(att_st, 0, turn)
    for turn in range(2):
        settle(g_s.at[turn], in_recv.at[3, turn])
        score_grads(turn)
        send_terms(turn)
        query_grads(turn)
        collect(dq_st, 1, turn)
    finish(0)
    finish(1)

    storing = [
        pltpu.make_async_copy(landed.at[n], out, store_sem.at[n])
        for n, out in enumerate((att_out, dq_out, dk_out, dv_out))
    ]
    most = pl.ds(0, 15 * DH)

    def settle_chunks(n, sem):
        pl.when(at_home)(lambda: settle(landed.at[n, :, most], sem))
        pl.when(jnp.logical_not(at_home))(lambda: settle(landed.at[n], sem))

    for n in (0, 1, 3, 2):
        settle_chunks(n, out_recv.at[n])
        storing[n].start()
    for n in range(4):
        settle_chunks(n, in_send.at[n])
        settle_chunks(n, out_send.at[n])
    for n in range(2):
        pl.when(has_far)(lambda n=n: settle(kw.at[0], halo_send.at[n, 0]))
        settle(kw.at[0], halo_send.at[n, 1])
        pl.when(has_far)(lambda n=n: settle(t_send.at[n, 0], term_send.at[n, 0]))
        settle(t_send.at[n, 1], term_send.at[n, 1])
    for copy in storing:
        copy.wait()


def handover(*refs):
    sources, results, held, read_sem, write_sem = refs[:4], refs[4:8], refs[8], refs[9], refs[10]
    reads = [pltpu.make_async_copy(src, held.at[n], read_sem.at[n]) for n, src in enumerate(sources)]
    writes = [pltpu.make_async_copy(held.at[n], dst, write_sem.at[n]) for n, dst in enumerate(results)]
    for copy in reads:
        copy.start()
    for read, write in zip(reads, writes):
        read.wait()
        write.start()
    for copy in writes:
        copy.wait()


def on_device(query_rows, key_rows, value_rows, grad_out):
    dma = pltpu.SemaphoreType.DMA
    rows = pltpu.VMEM((4, ROWS, HEADS * DH), BF16)
    window = pltpu.VMEM((4, SEG, DH), BF16)
    pair = pltpu.VMEM((2, SEG, DH), BF16)
    square = pltpu.VMEM((2, 3, SEG, SEG), BF16)
    terms = pltpu.VMEM((2, 2, SEG, DH), BF16)
    out = jax.ShapeDtypeStruct(query_rows.shape, BF16)
    in_hbm = [pl.BlockSpec(memory_space=pltpu.HBM)] * 4
    parts = pl.pallas_call(
        kernel,
        out_shape=[out] * 4,
        in_specs=in_hbm,
        out_specs=in_hbm,
        scratch_shapes=[
            rows, rows, window, window, pair, pair, square, square, pair,
            pltpu.VMEM((2, SEG, DH), F32), pltpu.VMEM((2, SEG, 1), F32),
            pair, pair, pair, pair, terms, terms,
            dma((4,)), dma((4,)), dma((4,)), dma((4, 2)),
            dma((2, 2)), dma((2, 2)), dma((2, 2)), dma((2, 2)), dma((4,)), dma((4,)),
        ],
        compiler_params=pltpu.CompilerParams(
            collective_id=0, has_side_effects=True, vmem_limit_bytes=63 * 2**20
        ),
        cost_estimate=pl.CostEstimate(flops=2_400_000_000, bytes_accessed=2 * 2**20, transcendentals=1_600_000),
        name="window_attention",
    )(query_rows, key_rows, value_rows, grad_out)
    return pl.pallas_call(
        handover,
        out_shape=[out] * 4,
        in_specs=in_hbm,
        out_specs=in_hbm,
        scratch_shapes=[rows, dma((4,)), dma((4,))],
        compiler_params=pltpu.CompilerParams(vmem_limit_bytes=63 * 2**20),
        name="handover",
    )(*parts)


def solution(mesh):
    spec = P(("blk", "head"), None)
    return jax.shard_map(
        on_device, mesh=mesh, in_specs=(spec,) * 4, out_specs=(spec,) * 4, check_vma=False
    )
```

time: 52.2 us -> 41.9 us (0.80)
  the two profiles are of different devices: /device:TPU:8 before, /device:TPU:1 now
where the time goes in v2:
time: 41.9 us; the launch traced here: 41.7 us
  Pallas kernels  41.1 us (98%)
  between operations  0.64 us (2%)
    pallas_call x1, Pallas kernels, on_device(): pl.pallas_call(kernel, out_shape=[out] * 4, in_specs=in_hbm, out_specs=in...  39.1 us
    pallas_call x1, Pallas kernels, on_device(): pl.pallas_call(handover, out_shape=[out] * 4, in_specs=in_hbm, out_specs=...  1.98 us

profile of v2, /device:TPU:1, one launch (start us, length us, event | category | flops | bytes accessed | tf_op | source)
XLA Modules:
  0.0 41.7 jit_solution(14671499717042778052)
XLA Ops:
  0.6 39.1 %window_attention.1 = (bf16[64,2048]{1,0:T(8,128)(2,1)}, bf16[64,2048]{1,0:T(8,128)(2,1)}, bf16[64,2048]{1,0:T(8,128)(2,1)}, bf16[64,2048]{1,0:T(8,128)(2,1)}) custom-call(bf16[64,2048]{1,0:T(8,128)(2,1)} %q_in.1, bf16[64,2048]{1,0:T(8,128)(2,1)} %k_in.1, bf16[64,2048]{1,0:T(8,128)(2,1)} %v_in.1, bf16[64,2048]{1,0:T(8,128)(2,1)} %g_in.1), custom_call_target="tpu_custom_call" | custom-call | flops 2400000000 | bytes 2097152 | tf_op jit(solution)/shard_map/window_attention/pallas_call | solution.py:292
  39.7 2.0 %handover.1 = (bf16[64,2048]{1,0:T(8,128)(2,1)}, bf16[64,2048]{1,0:T(8,128)(2,1)}, bf16[64,2048]{1,0:T(8,128)(2,1)}, bf16[64,2048]{1,0:T(8,128)(2,1)}) custom-call(bf16[64,2048]{1,0:T(8,128)(2,1)} %get-tuple-element.8.refs_0_, bf16[64,2048]{1,0:T(8,128)(2,1)} %get-tuple-element.9.refs_1_, bf16[64,2048]{1,0:T(8,128)(2,1)} %get-tuple-element.10.refs_2_, ...), custom_call_target="tpu_custom_call" | custom-call | tf_op jit(solution)/shard_map/handover/pallas_call | solution.py:310

commit v3 on v2

--- a/solution.py
+++ b/solution.py
@@ -11,7 +11,8 @@
 HEADS = 16
 SEG = 512
 ROWS = 64
-Q_ROWS = 128
+Q_ROWS = 256
+GRANT = 52 * 2**20 + 7 * 2**17
 SCALE = 1.0 / math.sqrt(DH)
 SCALE_2 = SCALE * math.log2(math.e)
 BF16 = jnp.bfloat16
@@ -34,8 +35,8 @@
 
 def kernel(
     q_in, k_in, v_in, g_in, att_out, dq_out, dk_out, dv_out,
-    staged_in, landed, kw, vw, q_s, g_s, e_s, d_s, gp_s, att_f, inv_s, att_st, dq_st, dk_st, dv_st,
-    t_send, t_recv, stage_sem, store_sem,
+    staged_in, kw, vw, q_s, g_s, e_s, d_s, gp_t, att_f, inv_s, att_st, dq_st, dk_st, dv_st,
+    t_send, t_recv, stage_sem,
     in_send, in_recv, halo_send, halo_recv, term_send, term_recv, out_send, out_recv,
 ):
     head = lax.axis_index("head")
@@ -66,7 +67,7 @@
             there = ((y_lo + dy) % 2) * 4 + (x + dx) % 4
             yield {"blk": 4 * z + 2 * core + segs[turn], "head": there}, there, turn == 0 and (dy, dx) == (0, 0)
 
-    inputs = (k_in, v_in, q_in, g_in)
+    inputs, results = (k_in, v_in, q_in, g_in), (att_out, dq_out, dk_out, dv_out)
     staging = [pltpu.make_async_copy(src, staged_in.at[n], stage_sem.at[n]) for n, src in enumerate(inputs)]
     for copy in staging:
         copy.start()
@@ -88,8 +89,8 @@
     def _():
         kw[3 * core] = jnp.zeros((SEG, DH), BF16)
         vw[3 * core] = jnp.zeros((SEG, DH), BF16)
-        t_recv[0, 0] = jnp.zeros((SEG, DH), BF16)
-        t_recv[1, 0] = jnp.zeros((SEG, DH), BF16)
+        t_recv[0, 0] = jnp.zeros((DH, SEG), BF16)
+        t_recv[1, 0] = jnp.zeros((DH, SEG), BF16)
 
     pl.semaphore_wait(barrier, 17 + away - at_end)
 
@@ -134,14 +135,16 @@
             rows = pl.ds(pl.multiple_of(there * ROWS, ROWS), ROWS)
 
             def go(rows=rows, target=target):
-                remote(staged.at[turn, rows, :], landed.at[n, :, my_column], out_send.at[n], out_recv.at[n], target)
+                remote(staged.at[turn, rows, :], results[n].at[:, my_column], out_send.at[n], out_recv.at[n], target)
 
             if own:
                 pl.when(jnp.logical_not(at_home))(go)
 
                 @pl.when(at_home)
                 def _():
-                    landed[n, :, my_column] = staged[turn, my_rows, :]
+                    pltpu.make_async_copy(
+                        staged.at[turn, my_rows, :], results[n].at[:, my_column], out_recv.at[n]
+                    ).start()
             else:
                 go()
 
@@ -178,7 +181,7 @@
         for r in range(0, SEG, Q_ROWS):
             rows = pl.ds(r, Q_ROWS)
             scaled = (g_s[turn, rows, :].astype(F32) * inv_s[turn, rows, :]).astype(BF16)
-            gp_s[turn, rows, :] = scaled
+            gp_t[turn, :, rows] = scaled.T
             delta = jnp.sum(scaled.astype(F32) * att_f[turn, rows, :], axis=1, keepdims=True)
             for j in range(3):
                 dprobs = nt(scaled, vw[seg + j])
@@ -191,10 +194,10 @@
             dq_st[turn, rows, :] = sum(nn(d_s[turn, j, rows, :], kw[seg + j]) for j in range(3)).astype(BF16)
 
     def value_terms(pairs):
-        return (sum(nn(gp_s[turn].T, e_s[turn, j]) for turn, j in pairs) * (1.0 / SCALE)).T
+        return sum(nn(gp_t[turn], e_s[turn, j]) for turn, j in pairs) * (1.0 / SCALE)
 
     def key_terms(pairs):
-        return sum(nn(q_s[turn].T, d_s[turn, j]) for turn, j in pairs).T
+        return sum(nn(q_s[turn].T, d_s[turn, j]) for turn, j in pairs)
 
     def send_terms(turn):
         outer = (2 * core, 2 - 2 * core)[turn]
@@ -221,7 +224,7 @@
                 pl.when(has_far)(arrive)
             else:
                 arrive()
-            staged[turn] = (own + t_recv[n, turn].astype(F32)).astype(BF16)
+            staged[turn] = (own + t_recv[n, turn].astype(F32)).astype(BF16).T
             collect(staged, 2 + n, turn)
 
     for turn in (1, 0):
@@ -242,41 +245,29 @@
     finish(0)
     finish(1)
 
-    storing = [
-        pltpu.make_async_copy(landed.at[n], out, store_sem.at[n])
-        for n, out in enumerate((att_out, dq_out, dk_out, dv_out))
-    ]
     most = pl.ds(0, 15 * DH)
 
-    def settle_chunks(n, sem):
-        pl.when(at_home)(lambda: settle(landed.at[n, :, most], sem))
-        pl.when(jnp.logical_not(at_home))(lambda: settle(landed.at[n], sem))
-
-    for n in (0, 1, 3, 2):
-        settle_chunks(n, out_recv.at[n])
-        storing[n].start()
+    def sent(n, sem):
+        pl.when(at_home)(lambda: settle(staged_in.at[n, :, most], sem))
+        pl.when(jnp.logical_not(at_home))(lambda: settle(staged_in.at[n], sem))
+
     for n in range(4):
-        settle_chunks(n, in_send.at[n])
-        settle_chunks(n, out_send.at[n])
+        settle(results[n], out_recv.at[n])
+        sent(n, in_send.at[n])
+        sent(n, out_send.at[n])
     for n in range(2):
         pl.when(has_far)(lambda n=n: settle(kw.at[0], halo_send.at[n, 0]))
         settle(kw.at[0], halo_send.at[n, 1])
         pl.when(has_far)(lambda n=n: settle(t_send.at[n, 0], term_send.at[n, 0]))
         settle(t_send.at[n, 1], term_send.at[n, 1])
-    for copy in storing:
-        copy.wait()
 
 
 def handover(*refs):
-    sources, results, held, read_sem, write_sem = refs[:4], refs[4:8], refs[8], refs[9], refs[10]
-    reads = [pltpu.make_async_copy(src, held.at[n], read_sem.at[n]) for n, src in enumerate(sources)]
-    writes = [pltpu.make_async_copy(held.at[n], dst, write_sem.at[n]) for n, dst in enumerate(results)]
-    for copy in reads:
+    sources, results, sems = refs[:4], refs[4:8], refs[8]
+    copies = [pltpu.make_async_copy(src, dst, sems.at[n]) for n, (src, dst) in enumerate(zip(sources, results))]
+    for copy in copies:
         copy.start()
-    for read, write in zip(reads, writes):
-        read.wait()
-        write.start()
-    for copy in writes:
+    for copy in copies:
         copy.wait()
 
 
@@ -286,7 +277,8 @@
     window = pltpu.VMEM((4, SEG, DH), BF16)
     pair = pltpu.VMEM((2, SEG, DH), BF16)
     square = pltpu.VMEM((2, 3, SEG, SEG), BF16)
-    terms = pltpu.VMEM((2, 2, SEG, DH), BF16)
+    turned = pltpu.VMEM((2, DH, SEG), BF16)
+    terms = pltpu.VMEM((2, 2, DH, SEG), BF16)
     out = jax.ShapeDtypeStruct(query_rows.shape, BF16)
     in_hbm = [pl.BlockSpec(memory_space=pltpu.HBM)] * 4
     parts = pl.pallas_call(
@@ -295,14 +287,14 @@
         in_specs=in_hbm,
         out_specs=in_hbm,
         scratch_shapes=[
-            rows, rows, window, window, pair, pair, square, square, pair,
+            rows, window, window, pair, pair, square, square, turned,
             pltpu.VMEM((2, SEG, DH), F32), pltpu.VMEM((2, SEG, 1), F32),
             pair, pair, pair, pair, terms, terms,
-            dma((4,)), dma((4,)), dma((4,)), dma((4, 2)),
+            dma((4,)), dma((4,)), dma((4, 2)),
             dma((2, 2)), dma((2, 2)), dma((2, 2)), dma((2, 2)), dma((4,)), dma((4,)),
         ],
         compiler_params=pltpu.CompilerParams(
-            collective_id=0, has_side_effects=True, vmem_limit_bytes=63 * 2**20
+            collective_id=0, has_side_effects=True, vmem_limit_bytes=GRANT
         ),
         cost_estimate=pl.CostEstimate(flops=2_400_000_000, bytes_accessed=2 * 2**20, transcendentals=1_600_000),
         name="window_attention",
@@ -312,8 +304,8 @@
         out_shape=[out] * 4,
         in_specs=in_hbm,
         out_specs=in_hbm,
-        scratch_shapes=[rows, dma((4,)), dma((4,))],
-        compiler_params=pltpu.CompilerParams(vmem_limit_bytes=63 * 2**20),
+        scratch_shapes=[dma((4,))],
+        compiler_params=pltpu.CompilerParams(vmem_limit_bytes=GRANT),
         name="handover",
     )(*parts)
 

time: 41.9 us -> 39.4 us (0.940)
  Pallas kernels: 41.1 us -> 38.6 us
    pallas_call x1, Pallas kernels: 39.1 us -> 37.6 us  [on_device(): pl.pallas_call(kernel, out_shape=[out] * 4, in_specs=in_hbm, out_specs=in...]
    pallas_call x1, Pallas kernels: 1.98 us -> 1 us  [on_device(): pl.pallas_call(handover, out_shape=[out] * 4, in_specs=in_hbm, out_specs=...]
where the time goes in v3:
time: 39.4 us; the launch traced here: 39.2 us
  Pallas kernels  38.6 us (98%)
  between operations  0.64 us (2%)
    pallas_call x1, Pallas kernels, on_device(): pl.pallas_call(kernel, out_shape=[out] * 4, in_specs=in_hbm, out_specs=in...  37.6 us
    pallas_call x1, Pallas kernels, on_device(): pl.pallas_call(handover, out_shape=[out] * 4, in_specs=in_hbm, out_specs=...  1 us

profile of v3, /device:TPU:1, one launch (start us, length us, event | category | flops | bytes accessed | tf_op | source)
XLA Modules:
  0.0 39.2 jit_solution(3146635873309341188)
XLA Ops:
  0.6 37.6 %window_attention.1 = (bf16[64,2048]{1,0:T(8,128)(2,1)S(1)}, bf16[64,2048]{1,0:T(8,128)(2,1)S(1)}, bf16[64,2048]{1,0:T(8,128)(2,1)S(1)}, bf16[64,2048]{1,0:T(8,128)(2,1)S(1)}) custom-call(bf16[64,2048]{1,0:T(8,128)(2,1)} %q_in.1, bf16[64,2048]{1,0:T(8,128)(2,1)} %k_in.1, bf16[64,2048]{1,0:T(8,128)(2,1)} %v_in.1, bf16[64,2048]{1,0:T(8,128)(2,1)} %g_in.1), custom_call_target="tpu_custom_call" | custom-call | flops 2400000000 | bytes 2097152 | tf_op jit(solution)/shard_map/window_attention/pallas_call | solution.py:284
  38.2 1.0 %handover.1 = (bf16[64,2048]{1,0:T(8,128)(2,1)}, bf16[64,2048]{1,0:T(8,128)(2,1)}, bf16[64,2048]{1,0:T(8,128)(2,1)}, bf16[64,2048]{1,0:T(8,128)(2,1)}) custom-call(bf16[64,2048]{1,0:T(8,128)(2,1)S(1)} %get-tuple-element.8.refs_0_, bf16[64,2048]{1,0:T(8,128)(2,1)S(1)} %get-tuple-element.9.refs_1_, bf16[64,2048]{1,0:T(8,128)(2,1)S(1)} %get-tuple-element.10.refs_2_, ...), custom_call_target="tpu_custom_call" | custom-call | tf_op jit(solution)/shard_map/handover/pallas_call | solution.py:302

commit v4 on v3

--- a/solution.py
+++ b/solution.py
@@ -35,8 +35,8 @@
 
 def kernel(
     q_in, k_in, v_in, g_in, att_out, dq_out, dk_out, dv_out,
-    staged_in, kw, vw, q_s, g_s, e_s, d_s, gp_t, att_f, inv_s, att_st, dq_st, dk_st, dv_st,
-    t_send, t_recv, stage_sem,
+    kw, vw, q_s, g_s, e_s, d_s, gp_t, att_f, inv_s, att_st, dq_st, dk_st, dv_st,
+    t_send, t_recv,
     in_send, in_recv, halo_send, halo_recv, term_send, term_recv, out_send, out_recv,
 ):
     head = lax.axis_index("head")
@@ -68,9 +68,6 @@
             yield {"blk": 4 * z + 2 * core + segs[turn], "head": there}, there, turn == 0 and (dy, dx) == (0, 0)
 
     inputs, results = (k_in, v_in, q_in, g_in), (att_out, dq_out, dk_out, dv_out)
-    staging = [pltpu.make_async_copy(src, staged_in.at[n], stage_sem.at[n]) for n, src in enumerate(inputs)]
-    for copy in staging:
-        copy.start()
     barrier = pltpu.get_barrier_semaphore()
 
     def greet(target):
@@ -99,14 +96,13 @@
 
     def spread(n, landing):
         send, recv = in_send.at[n], in_recv.at[n, away]
-        staging[n].wait()
         for dy, dx in PLANE:
             there_y, there_x = (y + dy) % 4, (x + dx) % 4
             columns = pl.ds(pl.multiple_of((4 * there_y + there_x) * DH, DH), DH)
             target = {"blk": 4 * z + 2 * (there_y // 2) + y_hi, "head": (there_y % 2) * 4 + there_x}
 
             def go(columns=columns, target=target):
-                remote(staged_in.at[n, :, columns], landing, send, recv, target)
+                remote(inputs[n].at[:, columns], landing, send, recv, target)
 
             if (dy, dx) == (0, 0):
                 pl.when(jnp.logical_not(at_home))(go)
@@ -239,17 +235,17 @@
     for turn in range(2):
         settle(g_s.at[turn], in_recv.at[3, turn])
         score_grads(turn)
-        send_terms(turn)
         query_grads(turn)
         collect(dq_st, 1, turn)
+        send_terms(turn)
     finish(0)
     finish(1)
 
     most = pl.ds(0, 15 * DH)
 
     def sent(n, sem):
-        pl.when(at_home)(lambda: settle(staged_in.at[n, :, most], sem))
-        pl.when(jnp.logical_not(at_home))(lambda: settle(staged_in.at[n], sem))
+        pl.when(at_home)(lambda: settle(results[n].at[:, most], sem))
+        pl.when(jnp.logical_not(at_home))(lambda: settle(results[n], sem))
 
     for n in range(4):
         settle(results[n], out_recv.at[n])
@@ -273,7 +269,6 @@
 
 def on_device(query_rows, key_rows, value_rows, grad_out):
     dma = pltpu.SemaphoreType.DMA
-    rows = pltpu.VMEM((4, ROWS, HEADS * DH), BF16)
     window = pltpu.VMEM((4, SEG, DH), BF16)
     pair = pltpu.VMEM((2, SEG, DH), BF16)
     square = pltpu.VMEM((2, 3, SEG, SEG), BF16)
@@ -287,10 +282,10 @@
         in_specs=in_hbm,
         out_specs=in_hbm,
         scratch_shapes=[
-            rows, window, window, pair, pair, square, square, turned,
+            window, window, pair, pair, square, square, turned,
             pltpu.VMEM((2, SEG, DH), F32), pltpu.VMEM((2, SEG, 1), F32),
             pair, pair, pair, pair, terms, terms,
-            dma((4,)), dma((4,)), dma((4, 2)),
+            dma((4,)), dma((4, 2)),
             dma((2, 2)), dma((2, 2)), dma((2, 2)), dma((2, 2)), dma((4,)), dma((4,)),
         ],
         compiler_params=pltpu.CompilerParams(

time: 39.4 us -> 39 us (0.990)
  Pallas kernels: 38.6 us -> 38.1 us
    pallas_call x1, Pallas kernels: 37.6 us -> 37.1 us  [on_device(): pl.pallas_call(kernel, out_shape=[out] * 4, in_specs=in_hbm, out_specs=in...]
where the time goes in v4:
time: 39 us; the launch traced here: 38.7 us
  Pallas kernels  38.1 us (98%)
  between operations  0.64 us (2%)
    pallas_call x1, Pallas kernels, on_device(): pl.pallas_call(kernel, out_shape=[out] * 4, in_specs=in_hbm, out_specs=in...  37.1 us
    pallas_call x1, Pallas kernels, on_device(): pl.pallas_call(handover, out_shape=[out] * 4, in_specs=in_hbm, out_specs=...  1 us

profile of v4, /device:TPU:1, one launch (start us, length us, event | category | flops | bytes accessed | tf_op | source)
XLA Modules:
  0.0 38.7 jit_solution(10713871280903069781)
XLA Ops:
  0.6 37.1 %window_attention.1 = (bf16[64,2048]{1,0:T(8,128)(2,1)S(1)}, bf16[64,2048]{1,0:T(8,128)(2,1)S(1)}, bf16[64,2048]{1,0:T(8,128)(2,1)S(1)}, bf16[64,2048]{1,0:T(8,128)(2,1)S(1)}) custom-call(bf16[64,2048]{1,0:T(8,128)(2,1)} %q_in.1, bf16[64,2048]{1,0:T(8,128)(2,1)} %k_in.1, bf16[64,2048]{1,0:T(8,128)(2,1)} %v_in.1, bf16[64,2048]{1,0:T(8,128)(2,1)} %g_in.1), custom_call_target="tpu_custom_call" | custom-call | flops 2400000000 | bytes 2097152 | tf_op jit(solution)/shard_map/window_attention/pallas_call | solution.py:279
  37.7 1.0 %handover.1 = (bf16[64,2048]{1,0:T(8,128)(2,1)}, bf16[64,2048]{1,0:T(8,128)(2,1)}, bf16[64,2048]{1,0:T(8,128)(2,1)}, bf16[64,2048]{1,0:T(8,128)(2,1)}) custom-call(bf16[64,2048]{1,0:T(8,128)(2,1)S(1)} %get-tuple-element.8.refs_0_, bf16[64,2048]{1,0:T(8,128)(2,1)S(1)} %get-tuple-element.9.refs_1_, bf16[64,2048]{1,0:T(8,128)(2,1)S(1)} %get-tuple-element.10.refs_2_, ...), custom_call_target="tpu_custom_call" | custom-call | tf_op jit(solution)/shard_map/handover/pallas_call | solution.py:297
